TPU v7x, 256 devices: a whole 4x4x8 slice. The times are simulated.
256 devices in a mesh: pop: 64 (over z, y_lo, x), wa: 4 (over y_hi, core).
Axes of the slice: x: 4, y: 4 (y_hi: 2, y_lo: 2; y = y_hi * 2 + y_lo), z: 8, core: 2. Of those that a mesh axis runs over, the one named last changes fastest.
Arguments:
- left_factors: bfloat16 [24576, 4, 1024], P('pop', None, 'wa'), may hold values from -16 to 16
- right_factors: bfloat16 [24576, 4, 4096], P('pop', None, 'wa'), may hold values from -6 to 6
- fitness_rank: int32 [24576], P('pop'), may hold values from 0 to 24575, each once
- sign_index: int32 [24576], P('pop'), may hold values 0 or 1
- master: float32 [1024, 4096], P(('wa', 'pop')), may hold values from -6 to 6
- moment: float32 [1024, 4096], P(('wa', 'pop')), may hold values from -6 to 6
- second: float32 [1024, 4096], P(('wa', 'pop')), may hold values from 0.5 to 2
Outputs:
- new_master: float32 [1024, 4096], P(('wa', 'pop'))
- new_moment: float32 [1024, 4096], P(('wa', 'pop'))
- new_second: float32 [1024, 4096], P(('wa', 'pop'))
- weights: bfloat16 [1024, 4096], P('wa')
Inputs may be any that keep to these rules, and one draw needn't show every extreme that they name: fitness_rank holds each of 0 to 24575 once.
All inputs are finite; a program needn't handle non-finite values. No bound on the sum of `sign_index` on one device may be relied on, other than what follows from the above.
Results may differ from a plain program's by a relative error of at most 0.0023.
Values may be sent and summed in bfloat16 or wider, within the bound.
A program may use at most 64 MiB of HBM per device.

v0:
```python
import jax
import jax.numpy as jnp
from jax import lax
from jax.sharding import PartitionSpec as P

R = 4
STEP = 3


def per_device(left_factors, right_factors, fitness_rank, sign_index, master, moment, second):
    members = left_factors.shape[0]
    rows_local = left_factors.shape[2]
    cols_local = right_factors.shape[2]
    pop_count = lax.axis_size("pop")
    wa_count = lax.axis_size("wa")
    population = members * pop_count
    square_sum = population * (population + 1) / (3.0 * (population - 1))
    fitness = (2.0 * fitness_rank.astype(jnp.float32) / (population - 1) - 1.0) * (
        1.0 - 2.0 * sign_index.astype(jnp.float32)
    )
    fitness = fitness / jnp.sqrt(jnp.float32(square_sum * R))
    scaled = (
        (left_factors * fitness[:, None, None])
        .astype(jnp.bfloat16)
        .reshape(members * R, rows_local)
    )
    whole_right = lax.all_gather(right_factors, "wa", axis=2, tiled=True).reshape(
        members * R, cols_local * wa_count
    )
    gradient = lax.psum_scatter(
        lax.dot_general(
            scaled, whole_right, (((0,), (0,)), ((), ())), preferred_element_type=jnp.float32
        ),
        "pop",
        scatter_dimension=0,
        tiled=True,
    )
    new_moment = 0.8 * moment + 0.2 * gradient
    new_second = 0.95 * second + 0.05 * gradient * gradient
    correct_one = 1.0 - 0.8**STEP
    correct_two = 1.0 - 0.95**STEP
    new_master = master - 0.3 * (new_moment / correct_one) / (
        jnp.sqrt(new_second / correct_two) + 1e-08
    )
    weights = lax.all_gather(new_master.astype(jnp.bfloat16), "pop", axis=0, tiled=True)
    return (new_master, new_moment, new_second, weights)


def solution(mesh):
    return jax.shard_map(
        per_device,
        mesh=mesh,
        in_specs=(
            P("pop", None, "wa"),
            P("pop", None, "wa"),
            P("pop"),
            P("pop"),
            P(("wa", "pop"), None),
            P(("wa", "pop"), None),
            P(("wa", "pop"), None),
        ),
        out_specs=(
            P(("wa", "pop"), None),
            P(("wa", "pop"), None),
            P(("wa", "pop"), None),
            P("wa", None),
        ),
        check_vma=False,
    )
```

profile of v0, /device:TPU:16, one launch (start us, length us, event | category | flops | bytes accessed | tf_op | source)
XLA Modules:
  0.0 1041.2 jit_solution(10484596904947684356)
XLA Ops:
  7.2 0.0 copy-start.4
  7.2 0.0 copy-start.5
  7.2 0.0 copy-start
  7.2 0.0 all-gather.4.cloned.1.call-start
  7.2 4.6 copy.13
  11.8 0.0 all-gather.4.cloned.1.call-update
  11.8 0.0 all-reduce.3.cloned.1.call-start
  11.9 0.0 copy-done.4
  11.9 0.0 copy-done.5
  11.9 0.0 copy-done
  11.9 0.5 multiply_convert_fusion
  12.4 88.4 %all-gather.4.cloned.1.call-done = bf16[384,4,4096]{2,0,1:T(8,128)(2,1)} async-done(((bf16[384,4,1024]{2,0,1:T(8,128)(2,1)}), bf16[384,4,4096]{2,0,1:T(8,128)(2,1)}) %all-gather.4.cloned.1.call-update) | async-done | bytes 12582928 | tf_op jit(solution)/shard_map/all_gather | solution.py:27
  100.8 9.5 convolution_bitcast_fusion
  110.3 0.0 copy-start.6
  110.3 0.0 copy-start.1
  110.3 0.0 copy-start.2
  110.3 0.0 copy-start.3
  110.3 0.0 all-reduce.3.cloned.1.call-update
  110.4 0.0 all-gather.6.cloned.1.call-start
  110.4 0.6 copy-done.6
  111.0 0.6 dynamic-slice
  112.2 618.9 %all-reduce.3.cloned.1.call-done = f32[256,4096]{1,0:T(8,128)} async-done(((f32[256,4096]{1,0:T(8,128)}), f32[256,4096]{1,0:T(8,128)}) %all-reduce.3.cloned.1.call-update) | async-done | bytes 4194320
  731.1 0.0 copy-done.1
  731.1 0.0 copy-done.2
  731.1 0.0 copy-done.3
  731.1 1.7 convert_bitcast_fusion
  732.8 0.0 all-gather.6.cloned.1.call-update
  732.8 297.9 %all-gather.6.cloned.1.call-done = bf16[64,4,4096]{2,1,0:T(4,128)(2,1)} async-done(((bf16[1,4,4096]{2,1,0:T(4,128)(2,1)}), bf16[64,4,4096]{2,1,0:T(4,128)(2,1)}) %all-gather.6.cloned.1.call-update) | async-done | bytes 2097168 | tf_op jit(solution)/shard_map/all_gather | solution.py:45
  1030.8 3.9 reshape.12
  (1 shorter events, 0.0 us)
Async XLA Ops:
  7.2 4.7 copy-start.4
  7.2 4.7 copy-start.5
  7.2 4.8 copy-start
  7.2 93.6 %all-gather.4.cloned.1.call-start = ((), (), s32[]{:S(2)}) async-start(), calls=%async_computation | async-start | bytes 15728640 | tf_op jit(solution)/shard_map/all_gather | solution.py:27
  11.8 719.3 %all-reduce.3.cloned.1.call-start = ((), (), s32[]{:S(2)}) async-start(), calls=%async_computation.2 | async-start | bytes 8388608
  110.3 0.7 copy-start.6
  110.3 620.8 %copy-start.1 = (f32[4,4096]{1,0:T(4,128)S(1)}, f32[4,4096]{1,0:T(4,128)}, u32[]{:S(2)}) copy-start(f32[4,4096]{1,0:T(4,128)} %param.11) | copy-start | bytes 196612
  110.3 620.8 %copy-start.2 = (f32[4,4096]{1,0:T(4,128)S(1)}, f32[4,4096]{1,0:T(4,128)}, u32[]{:S(2)}) copy-start(f32[4,4096]{1,0:T(4,128)} %param.12) | copy-start | bytes 196612
  110.3 620.8 %copy-start.3 = (f32[4,4096]{1,0:T(4,128)S(1)}, f32[4,4096]{1,0:T(4,128)}, u32[]{:S(2)}) copy-start(f32[4,4096]{1,0:T(4,128)} %param.13) | copy-start | bytes 196612
  110.4 920.4 %all-gather.6.cloned.1.call-start = ((), (), s32[]{:S(2)}) async-start(), calls=%async_computation.1 | async-start | bytes 2129920 | tf_op jit(solution)/shard_map/all_gather | solution.py:45
Sparse Core Ops, SparseCore 0:
  12.0 88.7 all-gather.3
  110.5 620.5 all-reduce.2
  733.6 297.0 all-gather.5
where the time goes:
time: 1040 us
  waiting for transfers between devices  1010 us (97%)
  between operations  14.5 us (1%)
    unnamed x4, waiting for transfers between devices  619 us
    all_gather x1, waiting for transfers between devices, per_device(): lax.all_gather(new_master.astype(jnp.bfloat16), 'pop', axis=0, tiled=True)  298 us
    all_gather x1, waiting for transfers between devices, per_device(): lax.all_gather(right_factors, 'wa', axis=2, tiled=True)  88.4 us
  transfers between devices with their start and end apart: 3, of which 3 were waited for; matrix products, arithmetic and copies ran while one was open for 0% of the time, Pallas kernels for 0%

commit v1 on v0

v1 whole, which is shorter than its diff:
```python
import math

import jax
import jax.numpy as jnp
from jax import lax
from jax.experimental import pallas as pl
from jax.experimental.pallas import tpu as pltpu
from jax.sharding import PartitionSpec as P

R = 4
STEP = 3
NZ, NYL, NX = 8, 2, 4
MESH = pl.DeviceIdType.MESH
F32 = jnp.float32
BF16 = jnp.bfloat16


def kernel(
    left_hbm, right_hbm, rank_ref, sign_ref, master_hbm, moment_hbm, second_hbm,
    out_master, out_moment, out_second, out_weights,
    left_raw, left_scaled, right, scale, adam_in,
    grad_p, grad_q, recv_p1, recv_p2, recv_q1, recv_q2, recv_y,
    state_send, state_recv, result_send, result_recv, rows_f32,
    gather_p, gather_q,
    send_sems, recv_sems, local_sems,
):
    members = rank_ref.shape[0]
    depth = members * R
    pop = lax.axis_index("pop")
    wa = lax.axis_index("wa")
    z, yl, x = pop // (NYL * NX), lax.rem(pop // NX, NYL), lax.rem(pop, NX)
    yh, core = wa // 2, lax.rem(wa, 2)
    population = members * NZ * NYL * NX

    def flip(bit, by):
        return 1 - bit if by else bit

    def device(z_, yl_, x_, yh_, core_):
        return (z_ * (NYL * NX) + yl_ * NX + x_, yh_ * 2 + core_)

    def z_peer(step):
        return device(lax.rem(z + step + NZ, NZ), yl, x, yh, core)

    def x_peer(step):
        return device(z, yl, lax.rem(x + step + NX, NX), yh, core)

    def y_peer(phase, part, half):
        return device(z, flip(yl, half), x, flip(yh, phase), flip(core, part))

    others = [(a, b, c) for a in range(2) for b in range(2) for c in range(2) if a + b + c]
    peers = [z_peer(1), z_peer(-1)] + [x_peer(k) for k in (1, 2, 3)]
    peers += [y_peer(*o) for o in others]

    messages = []

    def send(src, dst, to):
        index = len(messages)
        message = pltpu.make_async_remote_copy(
            src_ref=src, dst_ref=dst, send_sem=send_sems.at[index],
            recv_sem=recv_sems.at[index], device_id=to, device_id_type=MESH,
        )
        message.start()
        messages.append(message)
        return message

    left_view = left_hbm.reshape(depth, left_hbm.shape[2])
    right_view = right_hbm.reshape(depth, right_hbm.shape[2])
    load_left = pltpu.make_async_copy(left_view, left_raw.at[0], local_sems.at[0])
    load_left.start()
    load_right = []
    for c in range(NX):
        load_right.append(
            pltpu.make_async_copy(
                right_view.at[:, pl.ds(c * 256, 256)], right.at[c], local_sems.at[1 + c]
            )
        )
    load_state = [
        pltpu.make_async_copy(ref, adam_in.at[a], local_sems.at[5 + a])
        for a, ref in enumerate((master_hbm, moment_hbm, second_hbm))
    ]

    barrier = pltpu.get_barrier_semaphore()
    for peer in peers:
        pl.semaphore_signal(barrier, inc=1, device_id=peer, device_id_type=MESH)
    pl.semaphore_wait(barrier, len(peers))

    to_chip = send(left_view, left_raw.at[2], y_peer(1, 0, 0))
    to_core = send(left_view, left_raw.at[1], y_peer(0, 1, 0))
    for copy in load_right + load_state:
        copy.start()

    square_sum = population * (population + 1) / (3.0 * (population - 1))
    norm = 1.0 / ((population - 1) * math.sqrt(square_sum * R))
    upper = lax.broadcasted_iota(jnp.int32, (8, 128), 0) < R

    def fill(j, _):
        def centred(m):
            return (2 * rank_ref[m] - (population - 1)) * (1 - 2 * sign_ref[m])

        first, second_ = centred(2 * j), centred(2 * j + 1)
        both = jnp.where(upper, jnp.full((8, 128), first), jnp.full((8, 128), second_))
        scale[pl.ds(pl.multiple_of(8 * j, 8), 8), :] = both.astype(F32) * norm
        return 0

    lax.fori_loop(0, members // 2, fill, 0)

    def product(slot, phase, part):
        def scaling(k, _):
            rows = pl.ds(pl.multiple_of(k * 128, 128), 128)
            factor = scale[rows, :]
            for half in range(2):
                cols = pl.ds(half * 128, 128)
                left_scaled[slot, rows, cols] = (
                    left_raw[slot, rows, cols].astype(F32) * factor
                ).astype(BF16)
            return 0

        lax.fori_loop(0, depth // 128, scaling, 0)

        def columns(c, _):
            block = lax.dot_general(
                left_scaled[slot], right[c], (((0,), (0,)), ((), ())),
                preferred_element_type=F32,
            )
            for zz in range(NZ):
                for yy in range(NYL):
                    half = 1 - yl if yy else yl
                    at = zz * 32 + yy * 16
                    piece = block[at : at + 16, :]
                    if part == 0:
                        grad_p[phase, half, zz, c] = piece
                    else:
                        grad_q[phase, half, c, zz] = piece
            return 0

        lax.fori_loop(0, NX, columns, 0)

    def ring_sum(chunks, slots, first_slot, size, me, peer, half):
        long = 1 if half == 0 else -1
        lanes = []
        slot = first_slot
        for direction in (long, -long):
            steps = size // 2 if direction == long else size // 2 - 1
            lanes.append((direction, steps, slot))
            slot += steps
        pending = {}

        def chunk(direction, distance):
            return lax.rem(me + direction * distance + size, size)

        for direction, steps, slot in lanes:
            pending[direction] = send(
                chunks.at[chunk(direction, steps)], slots.at[slot], peer(direction)
            )
        yield
        for j in range(1, size // 2 + 1):
            for direction, steps, slot in lanes:
                if j > steps:
                    continue
                pending[direction].wait_recv()
                target = chunk(direction, steps - j)
                chunks[target] = chunks[target] + slots[slot + j - 1]
                if j < steps:
                    pending[direction] = send(
                        chunks.at[target], slots.at[slot + j], peer(direction)
                    )
            yield

    exchanged = {}

    def reduction(phase, part, half):
        if part == 0:
            own = grad_p.at[phase, half]
            yield from ring_sum(own, recv_p1.at[phase, half], 0, NZ, z, z_peer, half)
            own = own.at[z]
            yield from ring_sum(own, recv_p2.at[phase, half], 0, NX, x, x_peer, half)
            own = own.at[x]
        else:
            own = grad_q.at[phase, half]
            yield from ring_sum(own, recv_q1.at[phase, half], 0, NX, x, x_peer, half)
            own = own.at[x]
            yield from ring_sum(own, recv_q2.at[phase, half], 0, NZ, z, z_peer, half)
            own = own.at[z]
        if phase + part + half:
            exchanged[phase, part, half] = send(
                own, recv_y.at[phase, part, half], y_peer(phase, part, half)
            )

    def run(tasks):
        while tasks:
            alive = []
            for task in tasks:
                try:
                    next(task)
                    alive.append(task)
                except StopIteration:
                    pass
            tasks = alive

    def begin(phase, part):
        tasks = [reduction(phase, part, half) for half in range(2)]
        for task in tasks:
            next(task)
        return tasks

    load_left.wait()
    for copy in load_right:
        copy.wait()
    product(0, 0, 0)
    tasks = begin(0, 0)
    to_core.wait_recv()
    product(1, 0, 1)
    tasks += begin(0, 1)

    for copy in load_state:
        copy.wait()
    for xx in range(NX):
        for w in range(4):
            for a in range(3):
                state_send[xx, w, a] = adam_in[a, :, pl.ds(w * 1024 + xx * 256, 256)]
    state_recv[x] = state_send[x]
    state = []
    for k in (1, 2, 3):
        state.append(send(state_send.at[lax.rem(x + k, NX)], state_recv.at[x], x_peer(k)))

    to_chip.wait_recv()
    to_core2 = send(left_raw.at[2], left_raw.at[3], y_peer(0, 1, 0))
    run(tasks)
    product(2, 1, 0)
    tasks = begin(1, 0)
    to_core2.wait_recv()
    product(3, 1, 1)
    tasks += begin(1, 1)
    run(tasks)

    for message in state:
        message.wait_recv()
    for message in exchanged.values():
        message.wait_recv()
    correct_one = 1.0 - 0.8**STEP
    correct_two = 1.0 - 0.95**STEP
    gathered = []
    for phase in range(2):
        for part in range(2):
            owner = flip(yh, phase) * 2 + flip(core, part)
            if phase + part == 0:
                gradient = grad_p[0, 0, z, x]
            else:
                gradient = recv_y[phase, part, 0]
            gradient = gradient + recv_y[phase, part, 1]
            for xx in range(NX):
                g = gradient[4 * xx : 4 * xx + 4, :]
                old_master = state_recv[xx, owner, 0]
                old_moment = state_recv[xx, owner, 1]
                old_second = state_recv[xx, owner, 2]
                new_moment = 0.8 * old_moment + 0.2 * g
                new_second = 0.95 * old_second + 0.05 * g * g
                new_master = old_master - 0.3 * (new_moment / correct_one) / (
                    jnp.sqrt(new_second / correct_two) + 1e-08
                )
                result_send[xx, owner, 0] = new_master
                result_send[xx, owner, 1] = new_moment
                result_send[xx, owner, 2] = new_second
                rows_f32[4 * xx : 4 * xx + 4, :] = new_master
            rounded = rows_f32[...].astype(BF16)
            if phase == 0:
                own = gather_p.at[part, z, x, yl]
            else:
                own = gather_q.at[part, x, z, yl]
            own[...] = rounded
            gathered.append(send(own, own, y_peer(0, 0, 1)))

    result_recv[x] = result_send[x]

    def ring_gather(blocks, size, me, peer, half):
        long = 1 if half == 0 else -1
        lanes = [(long, size // 2), (-long, size // 2 - 1)]
        pending = {}
        for j in range(1, size // 2 + 1):
            for direction, steps in lanes:
                if j > steps:
                    continue
                if j > 1:
                    pending[direction].wait_recv()
                block = blocks.at[lax.rem(me - direction * (j - 1) + size, size)]
                pending[direction] = send(block, block, peer(direction))
            yield
        for message in pending.values():
            message.wait_recv()

    def gather(part, half):
        gathered[2 * part + half].wait_recv()
        if part == 0:
            blocks = gather_p.at[half]
            yield from ring_gather(blocks.at[z], NX, x, x_peer, half)
            yield from ring_gather(blocks, NZ, z, z_peer, half)
        else:
            blocks = gather_q.at[half]
            yield from ring_gather(blocks.at[x], NZ, z, z_peer, half)
            yield from ring_gather(blocks, NX, x, x_peer, half)

    tasks = [gather(part, half) for half in range(2) for part in range(2)]
    for task in tasks:
        next(task)
    result = []
    for k in (1, 2, 3):
        result.append(send(result_send.at[lax.rem(x + k, NX)], result_recv.at[x], x_peer(k)))
    run(tasks)

    for part in range(2):
        for half in range(2):
            owner = flip(yh, part) * 2 + flip(core, half)

            def place(zz, _):
                for xx in range(NX):
                    cols = pl.ds(pl.multiple_of(owner * 1024 + xx * 256, 256), 256)
                    for yy in range(NYL):
                        rows = pl.ds(pl.multiple_of(zz * 32 + yy * 16, 16), 16)
                        if part == 0:
                            out_weights[rows, cols] = gather_p[half, zz, xx, yy]
                        else:
                            out_weights[rows, cols] = gather_q[half, xx, zz, yy]
                return 0

            lax.fori_loop(0, NZ, place, 0)

    for message in result:
        message.wait_recv()
    for xx in range(NX):
        for w in range(4):
            cols = pl.ds(w * 1024 + xx * 256, 256)
            out_master[:, cols] = result_recv[xx, w, 0]
            out_moment[:, cols] = result_recv[xx, w, 1]
            out_second[:, cols] = result_recv[xx, w, 2]

    for message in messages:
        message.wait_send()


def per_device(left_factors, right_factors, fitness_rank, sign_index, master, moment, second):
    members = left_factors.shape[0]
    depth = members * R
    any_ = pl.BlockSpec(memory_space=pl.ANY)
    smem = pl.BlockSpec(memory_space=pltpu.SMEM)
    vmem = pl.BlockSpec(memory_space=pltpu.VMEM)
    return pl.pallas_call(
        kernel,
        out_shape=(
            jax.ShapeDtypeStruct(master.shape, F32),
            jax.ShapeDtypeStruct(master.shape, F32),
            jax.ShapeDtypeStruct(master.shape, F32),
            jax.ShapeDtypeStruct((256, 4096), BF16),
        ),
        in_specs=[any_, any_, smem, smem, any_, any_, any_],
        out_specs=(vmem, vmem, vmem, vmem),
        scratch_shapes=[
            pltpu.VMEM((4, depth, 256), BF16),
            pltpu.VMEM((4, depth, 256), BF16),
            pltpu.VMEM((NX, depth, 256), BF16),
            pltpu.VMEM((depth, 128), F32),
            pltpu.VMEM((3, 4, 4096), F32),
            pltpu.VMEM((2, 2, NZ, NX, 16, 256), F32),
            pltpu.VMEM((2, 2, NX, NZ, 16, 256), F32),
            pltpu.VMEM((2, 2, 7, NX, 16, 256), F32),
            pltpu.VMEM((2, 2, 3, 16, 256), F32),
            pltpu.VMEM((2, 2, 3, NZ, 16, 256), F32),
            pltpu.VMEM((2, 2, 7, 16, 256), F32),
            pltpu.VMEM((2, 2, 2, 16, 256), F32),
            pltpu.VMEM((NX, 4, 3, 4, 256), F32),
            pltpu.VMEM((NX, 4, 3, 4, 256), F32),
            pltpu.VMEM((NX, 4, 3, 4, 256), F32),
            pltpu.VMEM((NX, 4, 3, 4, 256), F32),
            pltpu.VMEM((16, 256), F32),
            pltpu.VMEM((2, NZ, NX, NYL, 16, 256), BF16),
            pltpu.VMEM((2, NX, NZ, NYL, 16, 256), BF16),
            pltpu.SemaphoreType.DMA((160,)),
            pltpu.SemaphoreType.DMA((160,)),
            pltpu.SemaphoreType.DMA((8,)),
        ],
        compiler_params=pltpu.CompilerParams(
            collective_id=0, has_side_effects=True, vmem_limit_bytes=48 << 20
        ),
    )(left_factors, right_factors, fitness_rank, sign_index, master, moment, second)


def solution(mesh):
    return jax.shard_map(
        per_device,
        mesh=mesh,
        in_specs=(
            P("pop", None, "wa"),
            P("pop", None, "wa"),
            P("pop"),
            P("pop"),
            P(("wa", "pop"), None),
            P(("wa", "pop"), None),
            P(("wa", "pop"), None),
        ),
        out_specs=(
            P(("wa", "pop"), None),
            P(("wa", "pop"), None),
            P(("wa", "pop"), None),
            P("wa", None),
        ),
        check_vma=False,
    )
```

time: 1040 us -> 123 us (0.12)
  the two profiles are of different devices: /device:TPU:16 before, /device:TPU:4 now
where the time goes in v1:
time: 123 us
  Pallas kernels  114 us (93%)
  local copies, waits for them, and re-layouts  8.21 us (7%)
    pallas_call x1, Pallas kernels, per_device(): pl.pallas_call(kernel, out_shape=(jax.ShapeDtypeStruct(master.shape, F32)...  114 us
    unnamed x16, local copies, waits for them, and re-layouts  8.21 us

profile of v1, /device:TPU:4, one launch (start us, length us, event | category | flops | bytes accessed | tf_op | source)
XLA Modules:
  0.0 122.7 jit_solution(12007869795433228989)
XLA Ops:
  0.6 0.0 copy-start
  0.6 1.1 copy-done
  1.8 0.0 copy-start.1
  1.8 0.8 copy-done.1
  2.6 0.0 copy-start.2
  2.6 0.8 copy-done.2
  3.4 0.0 copy-start.3
  3.4 0.8 copy-done.3
  4.3 0.0 copy-start.4
  4.3 0.7 copy-done.4
  5.0 0.0 copy-start.5
  5.0 0.7 copy-done.5
  5.7 113.8 %shard_map.102 = (f32[4,4096]{1,0:T(4,128)S(1)}, f32[4,4096]{1,0:T(4,128)S(1)}, f32[4,4096]{1,0:T(4,128)S(1)}, bf16[256,4096]{1,0:T(8,128)(2,1)S(1)}) custom-call(bf16[384,4,256]{2,1,0:T(4,128)(2,1)S(1)} %copy-done, bf16[384,4,1024]{2,1,0:T(4,128)(2,1)} %right_hbm.1, s32[384]{0:T(512)S(1)} %copy-done.4, s32[384]{0:T(512)S(1)} %copy-done.5, ...), custom_call_target="tpu_custom_call" | custom-call | tf_op jit(solution)/shard_map/pallas_call | solution.py:346
  119.5 0.6 copy.15
  120.1 0.6 copy.16
  120.7 0.6 copy.17
  121.3 1.3 %copy.18 = bf16[256,4096]{1,0:T(8,128)(2,1)} copy(bf16[256,4096]{1,0:T(8,128)(2,1)S(1)} %get-tuple-element.11) | data formatting | bytes 4194304
Async XLA Ops:
  0.6 1.1 copy-start
  1.8 0.8 copy-start.1
  2.6 0.8 copy-start.2
  3.4 0.8 copy-start.3
  4.3 0.7 copy-start.4
  5.0 0.7 copy-start.5

commit v2 on v1

--- a/solution.py
+++ b/solution.py
@@ -16,15 +16,15 @@
 
 
 def kernel(
-    left_hbm, right_hbm, rank_ref, sign_ref, master_hbm, moment_hbm, second_hbm,
+    left_hbm, right_hbm, rank_hbm, sign_hbm, master_hbm, moment_hbm, second_hbm,
     out_master, out_moment, out_second, out_weights,
-    left_raw, left_scaled, right, scale, adam_in,
+    rank_ref, sign_ref, left_raw, left_scaled, right, scale, adam_in,
     grad_p, grad_q, recv_p1, recv_p2, recv_q1, recv_q2, recv_y,
     state_send, state_recv, result_send, result_recv, rows_f32,
     gather_p, gather_q,
     send_sems, recv_sems, local_sems,
 ):
-    members = rank_ref.shape[0]
+    members = rank_hbm.shape[0]
     depth = members * R
     pop = lax.axis_index("pop")
     wa = lax.axis_index("wa")
@@ -48,8 +48,13 @@
         return device(z, flip(yl, half), x, flip(yh, phase), flip(core, part))
 
     others = [(a, b, c) for a in range(2) for b in range(2) for c in range(2) if a + b + c]
-    peers = [z_peer(1), z_peer(-1)] + [x_peer(k) for k in (1, 2, 3)]
-    peers += [y_peer(*o) for o in others]
+    plane = [(k, flip_y) for flip_y in range(2) for k in (2, 1, 3, 0) if k + flip_y]
+
+    def plane_peer(k, flip_y):
+        return device(z, flip(yl, flip_y), lax.rem(x + k, NX), yh, core)
+
+    peers = [y_peer(*o) for o in others] + [z_peer(k) for k in range(1, NZ)]
+    peers += [plane_peer(*o) for o in plane if o[0]]
 
     messages = []
 
@@ -67,6 +72,10 @@
     right_view = right_hbm.reshape(depth, right_hbm.shape[2])
     load_left = pltpu.make_async_copy(left_view, left_raw.at[0], local_sems.at[0])
     load_left.start()
+    load_fitness = [
+        pltpu.make_async_copy(rank_hbm, rank_ref, local_sems.at[8]),
+        pltpu.make_async_copy(sign_hbm, sign_ref, local_sems.at[9]),
+    ]
     load_right = []
     for c in range(NX):
         load_right.append(
@@ -79,6 +88,9 @@
         for a, ref in enumerate((master_hbm, moment_hbm, second_hbm))
     ]
 
+    for copy in load_fitness + load_right + load_state:
+        copy.start()
+
     barrier = pltpu.get_barrier_semaphore()
     for peer in peers:
         pl.semaphore_signal(barrier, inc=1, device_id=peer, device_id_type=MESH)
@@ -86,8 +98,8 @@
 
     to_chip = send(left_view, left_raw.at[2], y_peer(1, 0, 0))
     to_core = send(left_view, left_raw.at[1], y_peer(0, 1, 0))
-    for copy in load_right + load_state:
-        copy.start()
+    for copy in load_fitness:
+        copy.wait()
 
     square_sum = population * (population + 1) / (3.0 * (population - 1))
     norm = 1.0 / ((population - 1) * math.sqrt(square_sum * R))
@@ -166,6 +178,20 @@
                     )
             yield
 
+    def direct_sum(chunks, slots, size, me, peer):
+        sent = []
+        for k in sorted(range(1, size), key=lambda k: -min(k, size - k)):
+            sent.append(
+                send(chunks.at[lax.rem(me + k, size)], slots.at[k - 1], peer(k))
+            )
+        yield
+        for message in sent:
+            message.wait_recv()
+        total = chunks[me]
+        for k in range(1, size):
+            total = total + slots[k - 1]
+        chunks[me] = total
+
     exchanged = {}
 
     def reduction(phase, part, half):
@@ -173,21 +199,22 @@
             own = grad_p.at[phase, half]
             yield from ring_sum(own, recv_p1.at[phase, half], 0, NZ, z, z_peer, half)
             own = own.at[z]
-            yield from ring_sum(own, recv_p2.at[phase, half], 0, NX, x, x_peer, half)
+            yield from direct_sum(own, recv_p2.at[phase, half], NX, x, x_peer)
             own = own.at[x]
         else:
             own = grad_q.at[phase, half]
             yield from ring_sum(own, recv_q1.at[phase, half], 0, NX, x, x_peer, half)
             own = own.at[x]
-            yield from ring_sum(own, recv_q2.at[phase, half], 0, NZ, z, z_peer, half)
+            yield from direct_sum(own, recv_q2.at[phase, half], NZ, z, z_peer)
             own = own.at[z]
         if phase + part + half:
             exchanged[phase, part, half] = send(
                 own, recv_y.at[phase, part, half], y_peer(phase, part, half)
             )
 
-    def run(tasks):
-        while tasks:
+    def run(tasks, rounds=None):
+        while tasks and rounds != 0:
+            rounds = None if rounds is None else rounds - 1
             alive = []
             for task in tasks:
                 try:
@@ -196,6 +223,7 @@
                 except StopIteration:
                     pass
             tasks = alive
+        return tasks
 
     def begin(phase, part):
         tasks = [reduction(phase, part, half) for half in range(2)]
@@ -223,15 +251,16 @@
     for k in (1, 2, 3):
         state.append(send(state_send.at[lax.rem(x + k, NX)], state_recv.at[x], x_peer(k)))
 
+    tasks = run(tasks, 5)
     to_chip.wait_recv()
     to_core2 = send(left_raw.at[2], left_raw.at[3], y_peer(0, 1, 0))
+    product(2, 1, 0)
+    later = begin(1, 0)
     run(tasks)
-    product(2, 1, 0)
-    tasks = begin(1, 0)
     to_core2.wait_recv()
     product(3, 1, 1)
-    tasks += begin(1, 1)
-    run(tasks)
+    later += begin(1, 1)
+    run(later)
 
     for message in state:
         message.wait_recv()
@@ -240,6 +269,7 @@
     correct_one = 1.0 - 0.8**STEP
     correct_two = 1.0 - 0.95**STEP
     gathered = []
+    gathered_z = []
     for phase in range(2):
         for part in range(2):
             owner = flip(yh, phase) * 2 + flip(core, part)
@@ -264,48 +294,52 @@
                 rows_f32[4 * xx : 4 * xx + 4, :] = new_master
             rounded = rows_f32[...].astype(BF16)
             if phase == 0:
-                own = gather_p.at[part, z, x, yl]
+                gather_p[z, x, yl, part] = rounded
             else:
-                own = gather_q.at[part, x, z, yl]
-            own[...] = rounded
-            gathered.append(send(own, own, y_peer(0, 0, 1)))
+                gather_q[x, yl, z, part] = rounded
+        if phase == 0:
+            own = gather_p.at[z, x, yl]
+            for k, flip_y in plane:
+                gathered.append(send(own, own, plane_peer(k, flip_y)))
+        else:
+            own = gather_q.at[x, yl, z]
+            for k in (4, 3, 5, 2, 6, 1, 7):
+                gathered_z.append(send(own, own, z_peer(k)))
 
     result_recv[x] = result_send[x]
 
-    def ring_gather(blocks, size, me, peer, half):
+    def ring_gather(half):
         long = 1 if half == 0 else -1
-        lanes = [(long, size // 2), (-long, size // 2 - 1)]
+        lanes = [(long, NZ // 2), (-long, NZ // 2 - 1)]
         pending = {}
-        for j in range(1, size // 2 + 1):
+        for j in range(1, NZ // 2 + 1):
             for direction, steps in lanes:
                 if j > steps:
                     continue
                 if j > 1:
                     pending[direction].wait_recv()
-                block = blocks.at[lax.rem(me - direction * (j - 1) + size, size)]
-                pending[direction] = send(block, block, peer(direction))
+                origin = lax.rem(z - direction * (j - 1) + NZ, NZ)
+                block = gather_p.at[origin, pl.ds(2 * half, 2)]
+                pending[direction] = send(block, block, z_peer(direction))
             yield
         for message in pending.values():
             message.wait_recv()
 
-    def gather(part, half):
-        gathered[2 * part + half].wait_recv()
-        if part == 0:
-            blocks = gather_p.at[half]
-            yield from ring_gather(blocks.at[z], NX, x, x_peer, half)
-            yield from ring_gather(blocks, NZ, z, z_peer, half)
-        else:
-            blocks = gather_q.at[half]
-            yield from ring_gather(blocks.at[x], NZ, z, z_peer, half)
-            yield from ring_gather(blocks, NX, x, x_peer, half)
-
-    tasks = [gather(part, half) for half in range(2) for part in range(2)]
+    for message in gathered:
+        message.wait_recv()
+    tasks = [ring_gather(half) for half in range(2)]
     for task in tasks:
         next(task)
+    for message in gathered_z:
+        message.wait_recv()
+    own = gather_q.at[x, yl]
+    gathered = [send(own, own, plane_peer(k, flip_y)) for k, flip_y in plane]
     result = []
     for k in (1, 2, 3):
         result.append(send(result_send.at[lax.rem(x + k, NX)], result_recv.at[x], x_peer(k)))
     run(tasks)
+    for message in gathered:
+        message.wait_recv()
 
     for part in range(2):
         for half in range(2):
@@ -317,9 +351,9 @@
                     for yy in range(NYL):
                         rows = pl.ds(pl.multiple_of(zz * 32 + yy * 16, 16), 16)
                         if part == 0:
-                            out_weights[rows, cols] = gather_p[half, zz, xx, yy]
+                            out_weights[rows, cols] = gather_p[zz, xx, yy, half]
                         else:
-                            out_weights[rows, cols] = gather_q[half, xx, zz, yy]
+                            out_weights[rows, cols] = gather_q[xx, yy, zz, half]
                 return 0
 
             lax.fori_loop(0, NZ, place, 0)
@@ -337,13 +371,26 @@
         message.wait_send()
 
 
+def write_out(*refs):
+    ins, outs, sems = refs[:4], refs[4:8], refs[8]
+    copies = [pltpu.make_async_copy(ins[i], outs[i], sems.at[i]) for i in range(4)]
+    for copy in reversed(copies):
+        copy.start()
+    for copy in copies:
+        copy.wait()
+
+
 def per_device(left_factors, right_factors, fitness_rank, sign_index, master, moment, second):
     members = left_factors.shape[0]
     depth = members * R
+    hbm = pl.BlockSpec(memory_space=pltpu.HBM)
     any_ = pl.BlockSpec(memory_space=pl.ANY)
-    smem = pl.BlockSpec(memory_space=pltpu.SMEM)
     vmem = pl.BlockSpec(memory_space=pltpu.VMEM)
-    return pl.pallas_call(
+    operands = [
+        pltpu.with_memory_space_constraint(a, pltpu.HBM)
+        for a in (left_factors, right_factors, fitness_rank, sign_index, master, moment, second)
+    ]
+    updated = pl.pallas_call(
         kernel,
         out_shape=(
             jax.ShapeDtypeStruct(master.shape, F32),
@@ -351,9 +398,11 @@
             jax.ShapeDtypeStruct(master.shape, F32),
             jax.ShapeDtypeStruct((256, 4096), BF16),
         ),
-        in_specs=[any_, any_, smem, smem, any_, any_, any_],
+        in_specs=[hbm] * 7,
         out_specs=(vmem, vmem, vmem, vmem),
         scratch_shapes=[
+            pltpu.SMEM((members,), jnp.int32),
+            pltpu.SMEM((members,), jnp.int32),
             pltpu.VMEM((4, depth, 256), BF16),
             pltpu.VMEM((4, depth, 256), BF16),
             pltpu.VMEM((NX, depth, 256), BF16),
@@ -371,16 +420,23 @@
             pltpu.VMEM((NX, 4, 3, 4, 256), F32),
             pltpu.VMEM((NX, 4, 3, 4, 256), F32),
             pltpu.VMEM((16, 256), F32),
-            pltpu.VMEM((2, NZ, NX, NYL, 16, 256), BF16),
-            pltpu.VMEM((2, NX, NZ, NYL, 16, 256), BF16),
-            pltpu.SemaphoreType.DMA((160,)),
-            pltpu.SemaphoreType.DMA((160,)),
-            pltpu.SemaphoreType.DMA((8,)),
+            pltpu.VMEM((NZ, NX, NYL, 2, 16, 256), BF16),
+            pltpu.VMEM((NX, NYL, NZ, 2, 16, 256), BF16),
+            pltpu.SemaphoreType.DMA((192,)),
+            pltpu.SemaphoreType.DMA((192,)),
+            pltpu.SemaphoreType.DMA((10,)),
         ],
         compiler_params=pltpu.CompilerParams(
             collective_id=0, has_side_effects=True, vmem_limit_bytes=48 << 20
         ),
-    )(left_factors, right_factors, fitness_rank, sign_index, master, moment, second)
+    )(*operands)
+    return pl.pallas_call(
+        write_out,
+        out_shape=tuple(jax.ShapeDtypeStruct(a.shape, a.dtype) for a in updated),
+        in_specs=[any_] * 4,
+        out_specs=(any_,) * 4,
+        scratch_shapes=[pltpu.SemaphoreType.DMA((4,))],
+    )(*updated)
 
 
 def solution(mesh):

time: 123 us -> 171 us (1.39)
  the two profiles are of different devices: /device:TPU:4 before, /device:TPU:32 now
where the time goes in v2:
time: 171 us
  Pallas kernels  167 us (98%)
  local copies, waits for them, and re-layouts  3.19 us (2%)
    pallas_call x1, Pallas kernels, per_device(): pl.pallas_call(kernel, out_shape=(jax.ShapeDtypeStruct(master.shape, F32)...  96.6 us
    pallas_call x1, Pallas kernels, per_device(): pl.pallas_call(write_out, out_shape=tuple((jax.ShapeDtypeStruct(a.shape,...  70.6 us

profile of v2, /device:TPU:32, one launch (start us, length us, event | category | flops | bytes accessed | tf_op | source)
XLA Modules:
  0.0 171.1 jit_solution(1792469286041383615)
XLA Ops:
  0.6 96.6 %shard_map.102 = (f32[4,4096]{1,0:T(4,128)S(1)}, f32[4,4096]{1,0:T(4,128)S(1)}, f32[4,4096]{1,0:T(4,128)S(1)}, bf16[256,4096]{1,0:T(8,128)(2,1)S(1)}) custom-call(bf16[384,4,256]{2,1,0:T(4,128)(2,1)} %left_hbm.1, bf16[384,4,1024]{2,1,0:T(4,128)(2,1)} %right_hbm.1, s32[384]{0:T(512)} %rank_hbm.1, s32[384]{0:T(512)} %sign_hbm.1, f32[4,4096]{1,0:T(4,128)} %master_hbm.1, ...), custom_call_target="tpu_custom_call" | custom-call | tf_op jit(solution)/shard_map/pallas_call | solution.py:393
  97.3 0.0 copy-start
  97.3 1.3 copy-done
  98.6 0.0 copy-start.1
  98.6 0.6 copy-done.1
  99.2 0.0 copy-start.2
  99.2 0.6 copy-done.2
  99.9 0.0 copy-start.3
  99.9 0.6 copy-done.3
  100.5 70.6 %shard_map.103 = (f32[4,4096]{1,0:T(4,128)}, f32[4,4096]{1,0:T(4,128)}, f32[4,4096]{1,0:T(4,128)}, bf16[256,4096]{1,0:T(8,128)(2,1)}) custom-call(f32[4,4096]{1,0:T(4,128)} %copy-done.1, f32[4,4096]{1,0:T(4,128)} %copy-done.2, f32[4,4096]{1,0:T(4,128)} %copy-done.3, bf16[256,4096]{1,0:T(8,128)(2,1)} %copy-done), custom_call_target="tpu_custom_call" | custom-call | tf_op jit(solution)/shard_map/pallas_call | solution.py:433
Async XLA Ops:
  97.3 1.3 copy-start
  98.6 0.6 copy-start.1
  99.2 0.6 copy-start.2
  99.9 0.6 copy-start.3

commit v3 on v2

--- a/solution.py
+++ b/solution.py
@@ -96,7 +96,10 @@
         pl.semaphore_signal(barrier, inc=1, device_id=peer, device_id_type=MESH)
     pl.semaphore_wait(barrier, len(peers))
 
-    to_chip = send(left_view, left_raw.at[2], y_peer(1, 0, 0))
+    halves = [pl.ds(0, depth // 2), pl.ds(depth // 2, depth // 2)]
+    to_chip = [
+        send(left_view.at[rows], left_raw.at[2, rows], y_peer(1, 0, 0)) for rows in halves
+    ]
     to_core = send(left_view, left_raw.at[1], y_peer(0, 1, 0))
     for copy in load_fitness:
         copy.wait()
@@ -139,7 +142,7 @@
                     half = 1 - yl if yy else yl
                     at = zz * 32 + yy * 16
                     piece = block[at : at + 16, :]
-                    if part == 0:
+                    if part == phase:
                         grad_p[phase, half, zz, c] = piece
                     else:
                         grad_q[phase, half, c, zz] = piece
@@ -176,7 +179,8 @@
                     pending[direction] = send(
                         chunks.at[target], slots.at[slot + j], peer(direction)
                     )
-            yield
+            if j < size // 2:
+                yield
 
     def direct_sum(chunks, slots, size, me, peer):
         sent = []
@@ -195,7 +199,7 @@
     exchanged = {}
 
     def reduction(phase, part, half):
-        if part == 0:
+        if part == phase:
             own = grad_p.at[phase, half]
             yield from ring_sum(own, recv_p1.at[phase, half], 0, NZ, z, z_peer, half)
             own = own.at[z]
@@ -212,33 +216,23 @@
                 own, recv_y.at[phase, part, half], y_peer(phase, part, half)
             )
 
-    def run(tasks, rounds=None):
-        while tasks and rounds != 0:
-            rounds = None if rounds is None else rounds - 1
-            alive = []
-            for task in tasks:
-                try:
-                    next(task)
-                    alive.append(task)
-                except StopIteration:
-                    pass
-            tasks = alive
-        return tasks
+    def step(tasks):
+        for task in tasks:
+            next(task, None)
 
     def begin(phase, part):
         tasks = [reduction(phase, part, half) for half in range(2)]
-        for task in tasks:
-            next(task)
+        step(tasks)
         return tasks
 
     load_left.wait()
     for copy in load_right:
         copy.wait()
     product(0, 0, 0)
-    tasks = begin(0, 0)
+    p0 = begin(0, 0)
     to_core.wait_recv()
     product(1, 0, 1)
-    tasks += begin(0, 1)
+    q0 = begin(0, 1)
 
     for copy in load_state:
         copy.wait()
@@ -251,28 +245,34 @@
     for k in (1, 2, 3):
         state.append(send(state_send.at[lax.rem(x + k, NX)], state_recv.at[x], x_peer(k)))
 
-    tasks = run(tasks, 5)
-    to_chip.wait_recv()
-    to_core2 = send(left_raw.at[2], left_raw.at[3], y_peer(0, 1, 0))
+    for tasks in (p0, q0, p0, q0, p0, p0):
+        step(tasks)
+    to_core2 = []
+    for message, rows in zip(to_chip, halves):
+        message.wait_recv()
+        to_core2.append(
+            send(left_raw.at[2, rows], left_raw.at[3, rows], y_peer(0, 1, 0))
+        )
     product(2, 1, 0)
-    later = begin(1, 0)
-    run(tasks)
-    to_core2.wait_recv()
+    q1 = begin(1, 0)
+    step(q0)
+    step(p0)
+    for message in to_core2:
+        message.wait_recv()
     product(3, 1, 1)
-    later += begin(1, 1)
-    run(later)
+    p1 = begin(1, 1)
 
     for message in state:
-        message.wait_recv()
-    for message in exchanged.values():
         message.wait_recv()
     correct_one = 1.0 - 0.8**STEP
     correct_two = 1.0 - 0.95**STEP
-    gathered = []
-    gathered_z = []
-    for phase in range(2):
+
+    def update(phase):
         for part in range(2):
             owner = flip(yh, phase) * 2 + flip(core, part)
+            for half in range(2):
+                if phase + part + half:
+                    exchanged[phase, part, half].wait_recv()
             if phase + part == 0:
                 gradient = grad_p[0, 0, z, x]
             else:
@@ -297,16 +297,6 @@
                 gather_p[z, x, yl, part] = rounded
             else:
                 gather_q[x, yl, z, part] = rounded
-        if phase == 0:
-            own = gather_p.at[z, x, yl]
-            for k, flip_y in plane:
-                gathered.append(send(own, own, plane_peer(k, flip_y)))
-        else:
-            own = gather_q.at[x, yl, z]
-            for k in (4, 3, 5, 2, 6, 1, 7):
-                gathered_z.append(send(own, own, z_peer(k)))
-
-    result_recv[x] = result_send[x]
 
     def ring_gather(half):
         long = 1 if half == 0 else -1
@@ -325,23 +315,39 @@
         for message in pending.values():
             message.wait_recv()
 
-    for message in gathered:
-        message.wait_recv()
-    tasks = [ring_gather(half) for half in range(2)]
-    for task in tasks:
-        next(task)
-    for message in gathered_z:
+    def ring_p():
+        update(0)
+        own = gather_p.at[z, x, yl]
+        sent = [send(own, own, plane_peer(k, flip_y)) for k, flip_y in plane]
+        yield
+        for message in sent:
+            message.wait_recv()
+        tasks = [ring_gather(half) for half in range(2)]
+        for _ in range(NZ // 2):
+            step(tasks)
+            yield
+        step(tasks)
+
+    gather0 = [ring_p()]
+    for tasks in (gather0, q1, p1, gather0, p1, q1, gather0, p1, gather0, p1, q1, gather0, p1):
+        step(tasks)
+    update(1)
+    own = gather_q.at[x, yl, z]
+    sent = [send(own, own, z_peer(k)) for k in (4, 3, 5, 2, 6, 1, 7)]
+    result = []
+    for k in (1, 2, 3):
+        result.append(send(result_send.at[lax.rem(x + k, NX)], result_recv.at[x], x_peer(k)))
+    result_recv[x] = result_send[x]
+    for message in sent:
         message.wait_recv()
     own = gather_q.at[x, yl]
     gathered = [send(own, own, plane_peer(k, flip_y)) for k, flip_y in plane]
-    result = []
-    for k in (1, 2, 3):
-        result.append(send(result_send.at[lax.rem(x + k, NX)], result_recv.at[x], x_peer(k)))
-    run(tasks)
-    for message in gathered:
-        message.wait_recv()
+    step(gather0)
 
     for part in range(2):
+        if part == 1:
+            for message in gathered:
+                message.wait_recv()
         for half in range(2):
             owner = flip(yh, part) * 2 + flip(core, half)
 
@@ -436,6 +442,7 @@
         in_specs=[any_] * 4,
         out_specs=(any_,) * 4,
         scratch_shapes=[pltpu.SemaphoreType.DMA((4,))],
+        compiler_params=pltpu.CompilerParams(vmem_limit_bytes=1 << 20),
     )(*updated)
 
 

time: 171 us -> 102 us (0.60)
  the two profiles are of different devices: /device:TPU:32 before, /device:TPU:1 now
where the time goes in v3:
time: 102 us
  Pallas kernels  101 us (99%)
    pallas_call x1, Pallas kernels, per_device(): pl.pallas_call(kernel, out_shape=(jax.ShapeDtypeStruct(master.shape, F32)...  99.7 us

profile of v3, /device:TPU:1, one launch (start us, length us, event | category | flops | bytes accessed | tf_op | source)
XLA Modules:
  0.0 101.7 jit_solution(2370321303904556930)
XLA Ops:
  0.6 99.7 %shard_map.102 = (f32[4,4096]{1,0:T(4,128)S(1)}, f32[4,4096]{1,0:T(4,128)S(1)}, f32[4,4096]{1,0:T(4,128)S(1)}, bf16[256,4096]{1,0:T(8,128)(2,1)S(1)}) custom-call(bf16[384,4,256]{2,1,0:T(4,128)(2,1)} %left_hbm.1, bf16[384,4,1024]{2,1,0:T(4,128)(2,1)} %right_hbm.1, s32[384]{0:T(512)} %rank_hbm.1, s32[384]{0:T(512)} %sign_hbm.1, f32[4,4096]{1,0:T(4,128)} %master_hbm.1, ...), custom_call_target="tpu_custom_call" | custom-call | tf_op jit(solution)/shard_map/pallas_call | solution.py:399
  100.3 1.4 %shard_map.103 = (f32[4,4096]{1,0:T(4,128)}, f32[4,4096]{1,0:T(4,128)}, f32[4,4096]{1,0:T(4,128)}, bf16[256,4096]{1,0:T(8,128)(2,1)}) custom-call(f32[4,4096]{1,0:T(4,128)S(1)} %get-tuple-element.8.refs_0_, f32[4,4096]{1,0:T(4,128)S(1)} %get-tuple-element.9.refs_1_, f32[4,4096]{1,0:T(4,128)S(1)} %get-tuple-element.10.refs_2_, ...), custom_call_target="tpu_custom_call" | custom-call | tf_op jit(solution)/shard_map/pallas_call | solution.py:439

commit v4 on v3

--- a/solution.py
+++ b/solution.py
@@ -10,6 +10,7 @@
 R = 4
 STEP = 3
 NZ, NYL, NX = 8, 2, 4
+PLACE = [0, 1, 7, 2, 6, 3, 5, 4]
 MESH = pl.DeviceIdType.MESH
 F32 = jnp.float32
 BF16 = jnp.bfloat16
@@ -245,7 +246,7 @@
     for k in (1, 2, 3):
         state.append(send(state_send.at[lax.rem(x + k, NX)], state_recv.at[x], x_peer(k)))
 
-    for tasks in (p0, q0, p0, q0, p0, p0):
+    for tasks in (p0, q0, p0, q0, p0):
         step(tasks)
     to_core2 = []
     for message, rows in zip(to_chip, halves):
@@ -255,7 +256,6 @@
         )
     product(2, 1, 0)
     q1 = begin(1, 0)
-    step(q0)
     step(p0)
     for message in to_core2:
         message.wait_recv()
@@ -266,6 +266,16 @@
         message.wait_recv()
     correct_one = 1.0 - 0.8**STEP
     correct_two = 1.0 - 0.95**STEP
+
+    blocks = (gather_p, gather_q)
+    columns_sent = ({}, {})
+    result = []
+
+    def return_results(phase):
+        for k in (1, 2, 3):
+            to = result_recv.at[phase, x]
+            result.append(send(result_send.at[phase, lax.rem(x + k, NX)], to, x_peer(k)))
+        result_recv[phase, x] = result_send[phase, x]
 
     def update(phase):
         for part in range(2):
@@ -288,90 +298,72 @@
                 new_master = old_master - 0.3 * (new_moment / correct_one) / (
                     jnp.sqrt(new_second / correct_two) + 1e-08
                 )
-                result_send[xx, owner, 0] = new_master
-                result_send[xx, owner, 1] = new_moment
-                result_send[xx, owner, 2] = new_second
+                result_send[phase, xx, part, 0] = new_master
+                result_send[phase, xx, part, 1] = new_moment
+                result_send[phase, xx, part, 2] = new_second
                 rows_f32[4 * xx : 4 * xx + 4, :] = new_master
             rounded = rows_f32[...].astype(BF16)
-            if phase == 0:
-                gather_p[z, x, yl, part] = rounded
-            else:
-                gather_q[x, yl, z, part] = rounded
-
-    def ring_gather(half):
-        long = 1 if half == 0 else -1
-        lanes = [(long, NZ // 2), (-long, NZ // 2 - 1)]
-        pending = {}
-        for j in range(1, NZ // 2 + 1):
-            for direction, steps in lanes:
-                if j > steps:
-                    continue
-                if j > 1:
-                    pending[direction].wait_recv()
-                origin = lax.rem(z - direction * (j - 1) + NZ, NZ)
-                block = gather_p.at[origin, pl.ds(2 * half, 2)]
-                pending[direction] = send(block, block, z_peer(direction))
-            yield
-        for message in pending.values():
-            message.wait_recv()
-
-    def ring_p():
+            blocks[phase][x, yl, 0, part] = rounded
+        for k in (4, 3, 5, 2, 6, 1, 7):
+            own = blocks[phase].at[x, yl, 0]
+            to = blocks[phase].at[x, yl, PLACE.index(NZ - k)]
+            columns_sent[phase][NZ - k] = send(own, to, z_peer(k))
+
+    def spread(phase, first, count):
+        for distance in PLACE[first : first + count]:
+            if distance:
+                columns_sent[phase][distance].wait_recv()
+        own = blocks[phase].at[x, yl, pl.ds(first, count)]
+        return [send(own, own, plane_peer(k, flip_y)) for k, flip_y in plane]
+
+    def place(phase):
+        for part in range(2):
+            owner = flip(yh, phase) * 2 + flip(core, part)
+            for distance in range(NZ):
+                first_row = lax.rem(z + distance, NZ) * 32
+
+                def put(xx, _):
+                    cols = pl.ds(pl.multiple_of(owner * 1024 + xx * 256, 256), 256)
+                    for yy in range(NYL):
+                        rows = pl.ds(pl.multiple_of(first_row + yy * 16, 16), 16)
+                        block = blocks[phase][xx, yy, PLACE.index(distance), part]
+                        out_weights[rows, cols] = block
+                    return 0
+
+                lax.fori_loop(0, NX, put, 0)
+
+    def gather0():
         update(0)
-        own = gather_p.at[z, x, yl]
-        sent = [send(own, own, plane_peer(k, flip_y)) for k, flip_y in plane]
         yield
-        for message in sent:
-            message.wait_recv()
-        tasks = [ring_gather(half) for half in range(2)]
-        for _ in range(NZ // 2):
-            step(tasks)
-            yield
-        step(tasks)
-
-    gather0 = [ring_p()]
-    for tasks in (gather0, q1, p1, gather0, p1, q1, gather0, p1, gather0, p1, q1, gather0, p1):
+        gathered.extend(spread(0, 0, NZ))
+        return_results(0)
+
+    gathered = []
+    g0 = [gather0()]
+    for tasks in (q0, p0, q1, p1, g0, q1, p1, g0, p1, p1, q1, p1):
         step(tasks)
     update(1)
-    own = gather_q.at[x, yl, z]
-    sent = [send(own, own, z_peer(k)) for k in (4, 3, 5, 2, 6, 1, 7)]
-    result = []
-    for k in (1, 2, 3):
-        result.append(send(result_send.at[lax.rem(x + k, NX)], result_recv.at[x], x_peer(k)))
-    result_recv[x] = result_send[x]
-    for message in sent:
-        message.wait_recv()
-    own = gather_q.at[x, yl]
-    gathered = [send(own, own, plane_peer(k, flip_y)) for k, flip_y in plane]
-    step(gather0)
-
-    for part in range(2):
-        if part == 1:
-            for message in gathered:
-                message.wait_recv()
-        for half in range(2):
-            owner = flip(yh, part) * 2 + flip(core, half)
-
-            def place(zz, _):
-                for xx in range(NX):
-                    cols = pl.ds(pl.multiple_of(owner * 1024 + xx * 256, 256), 256)
-                    for yy in range(NYL):
-                        rows = pl.ds(pl.multiple_of(zz * 32 + yy * 16, 16), 16)
-                        if part == 0:
-                            out_weights[rows, cols] = gather_p[zz, xx, yy, half]
-                        else:
-                            out_weights[rows, cols] = gather_q[xx, yy, zz, half]
-                return 0
-
-            lax.fori_loop(0, NZ, place, 0)
+    last = spread(1, 0, 1)
+    last += spread(1, 1, 4)
+    last += spread(1, 5, 3)
+    return_results(1)
+    for message in gathered:
+        message.wait_recv()
+    place(0)
+    for message in last:
+        message.wait_recv()
+    place(1)
 
     for message in result:
         message.wait_recv()
     for xx in range(NX):
-        for w in range(4):
-            cols = pl.ds(w * 1024 + xx * 256, 256)
-            out_master[:, cols] = result_recv[xx, w, 0]
-            out_moment[:, cols] = result_recv[xx, w, 1]
-            out_second[:, cols] = result_recv[xx, w, 2]
+        for phase in range(2):
+            for part in range(2):
+                owner = flip(yh, phase) * 2 + flip(core, part)
+                cols = pl.ds(pl.multiple_of(owner * 1024 + xx * 256, 256), 256)
+                out_master[:, cols] = result_recv[phase, xx, part, 0]
+                out_moment[:, cols] = result_recv[phase, xx, part, 1]
+                out_second[:, cols] = result_recv[phase, xx, part, 2]
 
     for message in messages:
         message.wait_send()
@@ -423,10 +415,10 @@
             pltpu.VMEM((2, 2, 2, 16, 256), F32),
             pltpu.VMEM((NX, 4, 3, 4, 256), F32),
             pltpu.VMEM((NX, 4, 3, 4, 256), F32),
-            pltpu.VMEM((NX, 4, 3, 4, 256), F32),
-            pltpu.VMEM((NX, 4, 3, 4, 256), F32),
+            pltpu.VMEM((2, NX, 2, 3, 4, 256), F32),
+            pltpu.VMEM((2, NX, 2, 3, 4, 256), F32),
             pltpu.VMEM((16, 256), F32),
-            pltpu.VMEM((NZ, NX, NYL, 2, 16, 256), BF16),
+            pltpu.VMEM((NX, NYL, NZ, 2, 16, 256), BF16),
             pltpu.VMEM((NX, NYL, NZ, 2, 16, 256), BF16),
             pltpu.SemaphoreType.DMA((192,)),
             pltpu.SemaphoreType.DMA((192,)),

time: 102 us -> 90.9 us (0.89)
  Pallas kernels: 101 us -> 90.2 us
    pallas_call x1, Pallas kernels: 99.7 us -> 88.8 us  [per_device(): pl.pallas_call(kernel, out_shape=(jax.ShapeDtypeStruct(master.shape, F32)...]
where the time goes in v4:
time: 90.9 us
  Pallas kernels  90.2 us (99%)
    pallas_call x1, Pallas kernels, per_device(): pl.pallas_call(kernel, out_shape=(jax.ShapeDtypeStruct(master.shape, F32)...  88.8 us

profile of v4, /device:TPU:1, one launch (start us, length us, event | category | flops | bytes accessed | tf_op | source)
XLA Modules:
  0.0 90.9 jit_solution(14767255125479321758)
XLA Ops:
  0.6 88.8 %shard_map.102 = (f32[4,4096]{1,0:T(4,128)S(1)}, f32[4,4096]{1,0:T(4,128)S(1)}, f32[4,4096]{1,0:T(4,128)S(1)}, bf16[256,4096]{1,0:T(8,128)(2,1)S(1)}) custom-call(bf16[384,4,256]{2,1,0:T(4,128)(2,1)} %left_hbm.1, bf16[384,4,1024]{2,1,0:T(4,128)(2,1)} %right_hbm.1, s32[384]{0:T(512)} %rank_hbm.1, s32[384]{0:T(512)} %sign_hbm.1, f32[4,4096]{1,0:T(4,128)} %master_hbm.1, ...), custom_call_target="tpu_custom_call" | custom-call | tf_op jit(solution)/shard_map/pallas_call | solution.py:391
  89.4 1.4 %shard_map.103 = (f32[4,4096]{1,0:T(4,128)}, f32[4,4096]{1,0:T(4,128)}, f32[4,4096]{1,0:T(4,128)}, bf16[256,4096]{1,0:T(8,128)(2,1)}) custom-call(f32[4,4096]{1,0:T(4,128)S(1)} %get-tuple-element.8.refs_0_, f32[4,4096]{1,0:T(4,128)S(1)} %get-tuple-element.9.refs_1_, f32[4,4096]{1,0:T(4,128)S(1)} %get-tuple-element.10.refs_2_, ...), custom_call_target="tpu_custom_call" | custom-call | tf_op jit(solution)/shard_map/pallas_call | solution.py:431

commit v5 on v4

--- a/solution.py
+++ b/solution.py
@@ -246,7 +246,7 @@
     for k in (1, 2, 3):
         state.append(send(state_send.at[lax.rem(x + k, NX)], state_recv.at[x], x_peer(k)))
 
-    for tasks in (p0, q0, p0, q0, p0):
+    for tasks in (p0, q0, p0, q0):
         step(tasks)
     to_core2 = []
     for message, rows in zip(to_chip, halves):
@@ -340,12 +340,12 @@
 
     gathered = []
     g0 = [gather0()]
-    for tasks in (q0, p0, q1, p1, g0, q1, p1, g0, p1, p1, q1, p1):
+    for tasks in (p0, q0, p0, p1, q1, g0, p1, q1, g0, p1, p1, q1, p1):
         step(tasks)
     update(1)
     last = spread(1, 0, 1)
-    last += spread(1, 1, 4)
-    last += spread(1, 5, 3)
+    last += spread(1, 1, 2)
+    last += spread(1, 3, 5)
     return_results(1)
     for message in gathered:
         message.wait_recv()

time: 90.9 us -> 88.3 us (0.971)
  Pallas kernels: 90.2 us -> 87.5 us
    pallas_call x1, Pallas kernels: 88.8 us -> 86.1 us  [per_device(): pl.pallas_call(kernel, out_shape=(jax.ShapeDtypeStruct(master.shape, F32)...]
where the time goes in v5:
time: 88.3 us; the launch traced here: 88.2 us
  Pallas kernels  87.5 us (99%)
    pallas_call x1, Pallas kernels, per_device(): pl.pallas_call(kernel, out_shape=(jax.ShapeDtypeStruct(master.shape, F32)...  86.1 us

profile of v5, /device:TPU:1, one launch (start us, length us, event | category | flops | bytes accessed | tf_op | source)
XLA Modules:
  0.0 88.2 jit_solution(15131498280432600324)
XLA Ops:
  0.6 86.1 %shard_map.102 = (f32[4,4096]{1,0:T(4,128)S(1)}, f32[4,4096]{1,0:T(4,128)S(1)}, f32[4,4096]{1,0:T(4,128)S(1)}, bf16[256,4096]{1,0:T(8,128)(2,1)S(1)}) custom-call(bf16[384,4,256]{2,1,0:T(4,128)(2,1)} %left_hbm.1, bf16[384,4,1024]{2,1,0:T(4,128)(2,1)} %right_hbm.1, s32[384]{0:T(512)} %rank_hbm.1, s32[384]{0:T(512)} %sign_hbm.1, f32[4,4096]{1,0:T(4,128)} %master_hbm.1, ...), custom_call_target="tpu_custom_call" | custom-call | tf_op jit(solution)/shard_map/pallas_call | solution.py:391
  86.8 1.4 %shard_map.103 = (f32[4,4096]{1,0:T(4,128)}, f32[4,4096]{1,0:T(4,128)}, f32[4,4096]{1,0:T(4,128)}, bf16[256,4096]{1,0:T(8,128)(2,1)}) custom-call(f32[4,4096]{1,0:T(4,128)S(1)} %get-tuple-element.8.refs_0_, f32[4,4096]{1,0:T(4,128)S(1)} %get-tuple-element.9.refs_1_, f32[4,4096]{1,0:T(4,128)S(1)} %get-tuple-element.10.refs_2_, ...), custom_call_target="tpu_custom_call" | custom-call | tf_op jit(solution)/shard_map/pallas_call | solution.py:431

commit v6 on v5

--- a/solution.py
+++ b/solution.py
@@ -131,7 +131,7 @@
                 ).astype(BF16)
             return 0
 
-        lax.fori_loop(0, depth // 128, scaling, 0)
+        lax.fori_loop(0, depth // 128, scaling, 0, unroll=4)
 
         def columns(c, _):
             block = lax.dot_general(
@@ -149,7 +149,7 @@
                         grad_q[phase, half, c, zz] = piece
             return 0
 
-        lax.fori_loop(0, NX, columns, 0)
+        lax.fori_loop(0, NX, columns, 0, unroll=True)
 
     def ring_sum(chunks, slots, first_slot, size, me, peer, half):
         long = 1 if half == 0 else -1

time: 88.3 us -> 86.8 us (0.983)
  Pallas kernels: 87.5 us -> 86.1 us
    pallas_call x1, Pallas kernels: 86.1 us -> 84.7 us  [per_device(): pl.pallas_call(kernel, out_shape=(jax.ShapeDtypeStruct(master.shape, F32)...]
where the time goes in v6:
time: 86.8 us; the launch traced here: 86.7 us
  Pallas kernels  86.1 us (99%)
    pallas_call x1, Pallas kernels, per_device(): pl.pallas_call(kernel, out_shape=(jax.ShapeDtypeStruct(master.shape, F32)...  84.7 us

profile of v6, /device:TPU:1, one launch (start us, length us, event | category | flops | bytes accessed | tf_op | source)
XLA Modules:
  0.0 86.7 jit_solution(7545926765187497444)
XLA Ops:
  0.6 84.7 %shard_map.102 = (f32[4,4096]{1,0:T(4,128)S(1)}, f32[4,4096]{1,0:T(4,128)S(1)}, f32[4,4096]{1,0:T(4,128)S(1)}, bf16[256,4096]{1,0:T(8,128)(2,1)S(1)}) custom-call(bf16[384,4,256]{2,1,0:T(4,128)(2,1)} %left_hbm.1, bf16[384,4,1024]{2,1,0:T(4,128)(2,1)} %right_hbm.1, s32[384]{0:T(512)} %rank_hbm.1, s32[384]{0:T(512)} %sign_hbm.1, f32[4,4096]{1,0:T(4,128)} %master_hbm.1, ...), custom_call_target="tpu_custom_call" | custom-call | tf_op jit(solution)/shard_map/pallas_call | solution.py:391
  85.3 1.4 %shard_map.103 = (f32[4,4096]{1,0:T(4,128)}, f32[4,4096]{1,0:T(4,128)}, f32[4,4096]{1,0:T(4,128)}, bf16[256,4096]{1,0:T(8,128)(2,1)}) custom-call(f32[4,4096]{1,0:T(4,128)S(1)} %get-tuple-element.8.refs_0_, f32[4,4096]{1,0:T(4,128)S(1)} %get-tuple-element.9.refs_1_, f32[4,4096]{1,0:T(4,128)S(1)} %get-tuple-element.10.refs_2_, ...), custom_call_target="tpu_custom_call" | custom-call | tf_op jit(solution)/shard_map/pallas_call | solution.py:431

commit v7 on v6

--- a/solution.py
+++ b/solution.py
@@ -118,7 +118,7 @@
         scale[pl.ds(pl.multiple_of(8 * j, 8), 8), :] = both.astype(F32) * norm
         return 0
 
-    lax.fori_loop(0, members // 2, fill, 0)
+    lax.fori_loop(0, members // 2, fill, 0, unroll=8)
 
     def product(slot, phase, part):
         def scaling(k, _):
@@ -131,7 +131,7 @@
                 ).astype(BF16)
             return 0
 
-        lax.fori_loop(0, depth // 128, scaling, 0, unroll=4)
+        lax.fori_loop(0, depth // 128, scaling, 0, unroll=True)
 
         def columns(c, _):
             block = lax.dot_general(
@@ -330,7 +330,7 @@
                         out_weights[rows, cols] = block
                     return 0
 
-                lax.fori_loop(0, NX, put, 0)
+                lax.fori_loop(0, NX, put, 0, unroll=True)
 
     def gather0():
         update(0)

time: 86.8 us -> 86.8 us (level)
  no operation moved by 1% of the time
where the time goes in v7:
time: 86.8 us; the launch traced here: 86.7 us
  Pallas kernels  86.1 us (99%)
    pallas_call x1, Pallas kernels, per_device(): pl.pallas_call(kernel, out_shape=(jax.ShapeDtypeStruct(master.shape, F32)...  84.7 us

profile of v7, /device:TPU:1, one launch (start us, length us, event | category | flops | bytes accessed | tf_op | source)
XLA Modules:
  0.0 86.7 jit_solution(5195046703365819242)
XLA Ops:
  0.6 84.7 %shard_map.102 = (f32[4,4096]{1,0:T(4,128)S(1)}, f32[4,4096]{1,0:T(4,128)S(1)}, f32[4,4096]{1,0:T(4,128)S(1)}, bf16[256,4096]{1,0:T(8,128)(2,1)S(1)}) custom-call(bf16[384,4,256]{2,1,0:T(4,128)(2,1)} %left_hbm.1, bf16[384,4,1024]{2,1,0:T(4,128)(2,1)} %right_hbm.1, s32[384]{0:T(512)} %rank_hbm.1, s32[384]{0:T(512)} %sign_hbm.1, f32[4,4096]{1,0:T(4,128)} %master_hbm.1, ...), custom_call_target="tpu_custom_call" | custom-call | tf_op jit(solution)/shard_map/pallas_call | solution.py:391
  85.3 1.4 %shard_map.103 = (f32[4,4096]{1,0:T(4,128)}, f32[4,4096]{1,0:T(4,128)}, f32[4,4096]{1,0:T(4,128)}, bf16[256,4096]{1,0:T(8,128)(2,1)}) custom-call(f32[4,4096]{1,0:T(4,128)S(1)} %get-tuple-element.8.refs_0_, f32[4,4096]{1,0:T(4,128)S(1)} %get-tuple-element.9.refs_1_, f32[4,4096]{1,0:T(4,128)S(1)} %get-tuple-element.10.refs_2_, ...), custom_call_target="tpu_custom_call" | custom-call | tf_op jit(solution)/shard_map/pallas_call | solution.py:431

commit v8 on v7

--- a/solution.py
+++ b/solution.py
@@ -54,8 +54,9 @@
     def plane_peer(k, flip_y):
         return device(z, flip(yl, flip_y), lax.rem(x + k, NX), yh, core)
 
-    peers = [y_peer(*o) for o in others] + [z_peer(k) for k in range(1, NZ)]
-    peers += [plane_peer(*o) for o in plane if o[0]]
+    peers = [z_peer(k) for k in (4, 3, 5, 2, 6, 1, 7)]
+    peers += [plane_peer(*o) for o in reversed(plane) if o[0]]
+    peers += [y_peer(*o) for o in reversed(others)]
 
     messages = []
 

time: 86.8 us -> 86.7 us (level)
  no operation moved by 1% of the time
where the time goes in v8:
time: 86.7 us; the launch traced here: 86.6 us
  Pallas kernels  86 us (99%)
    pallas_call x1, Pallas kernels, per_device(): pl.pallas_call(kernel, out_shape=(jax.ShapeDtypeStruct(master.shape, F32)...  84.6 us

profile of v8, /device:TPU:1, one launch (start us, length us, event | category | flops | bytes accessed | tf_op | source)
XLA Modules:
  0.0 86.6 jit_solution(6549765426975204948)
XLA Ops:
  0.6 84.6 %shard_map.102 = (f32[4,4096]{1,0:T(4,128)S(1)}, f32[4,4096]{1,0:T(4,128)S(1)}, f32[4,4096]{1,0:T(4,128)S(1)}, bf16[256,4096]{1,0:T(8,128)(2,1)S(1)}) custom-call(bf16[384,4,256]{2,1,0:T(4,128)(2,1)} %left_hbm.1, bf16[384,4,1024]{2,1,0:T(4,128)(2,1)} %right_hbm.1, s32[384]{0:T(512)} %rank_hbm.1, s32[384]{0:T(512)} %sign_hbm.1, f32[4,4096]{1,0:T(4,128)} %master_hbm.1, ...), custom_call_target="tpu_custom_call" | custom-call | tf_op jit(solution)/shard_map/pallas_call | solution.py:392
  85.2 1.4 %shard_map.103 = (f32[4,4096]{1,0:T(4,128)}, f32[4,4096]{1,0:T(4,128)}, f32[4,4096]{1,0:T(4,128)}, bf16[256,4096]{1,0:T(8,128)(2,1)}) custom-call(f32[4,4096]{1,0:T(4,128)S(1)} %get-tuple-element.8.refs_0_, f32[4,4096]{1,0:T(4,128)S(1)} %get-tuple-element.9.refs_1_, f32[4,4096]{1,0:T(4,128)S(1)} %get-tuple-element.10.refs_2_, ...), custom_call_target="tpu_custom_call" | custom-call | tf_op jit(solution)/shard_map/pallas_call | solution.py:432
